TPU v7x, 256 devices: a whole 4x4x8 slice. The times are simulated.
256 devices in a mesh: island: 16 (over x, z_lo), expert: 4 (over y), fsdp: 4 (over z_hi, core).
Axes of the slice: x: 4, y: 4, z: 8 (z_hi: 2, z_lo: 4; z = z_hi * 4 + z_lo), core: 2. Of those that a mesh axis runs over, the one named last changes fastest.
Arguments:
- deltas: bfloat16 [16, 4, 4096, 1536], P('island', 'expert', 'fsdp'), may hold values from -6 to 6
- order: int32 [4], replicated, may hold values from 0 to 15
- staleness: int32 [16], replicated, may hold values from 0 to 15
- period: int32 [1], replicated, may hold values from 2 to 4
- counter: int32 [1], replicated, may hold values from 0 to 11
- theta: float32 [4, 4096, 1536], P('expert', ('fsdp', 'island')), may hold values from -6 to 6
- momentum: float32 [4, 4096, 1536], P('expert', ('fsdp', 'island')), may hold values from -4 to 4
- accum: float32 [4, 4096, 1536], P('expert', ('fsdp', 'island')), may hold values from -4 to 4
Outputs:
- fresh: bfloat16 [16, 4, 4096, 1536], P('island', 'expert', 'fsdp')
- theta_out: float32 [4, 4096, 1536], P('expert', ('fsdp', 'island'))
- momentum_out: float32 [4, 4096, 1536], P('expert', ('fsdp', 'island'))
- accum_out: float32 [4, 4096, 1536], P('expert', ('fsdp', 'island'))
All inputs are finite; a program needn't handle non-finite values.
Results may differ from a plain program's by a relative error of at most 0.001.
Values may be sent and summed in bfloat16 or wider, within the bound.
A program may use at most 128 MiB of HBM per device.

v0:
```python
import jax
import jax.numpy as jnp
from jax import lax
from jax.sharding import PartitionSpec as P


def spread(shard, axis, root):
    mine = lax.axis_index(axis) == root
    return lax.psum(jnp.where(mine, shard, jnp.zeros_like(shard)), axis)


def local(deltas, order, staleness, period, counter, theta, momentum, accum):
    rate = 0.7
    beta = 0.9
    islands = lax.axis_size("island")
    myself = lax.axis_index("island")
    mine = deltas[0]
    exp_loc, rows_all, width = mine.shape
    rows = rows_all // islands
    period_f = period[0].astype(jnp.float32)
    fresh = jnp.zeros(mine.shape, jnp.bfloat16)
    for k in range(order.shape[0]):
        source = order[k]
        whole = spread(mine, "island", source)
        piece = lax.dynamic_slice_in_dim(whole, myself * rows, rows, 1)
        weight = lax.rsqrt(1.0 + staleness[source].astype(jnp.float32) + k)
        grad = weight * piece.astype(jnp.float32)
        boundary = (counter[0] + k + 1) % period[0] == 0
        correction = 1.0 - jnp.power(jnp.float32(beta), (counter[0] + k + 1).astype(jnp.float32))
        momentum = jnp.where(boundary, beta * momentum + accum / period_f, momentum)
        accum = jnp.where(boundary, grad, accum + grad)
        theta = theta - rate * (
            grad + jnp.where(boundary, beta * momentum / correction, jnp.float32(0.0))
        )
        rounded = theta.astype(jnp.bfloat16)
        gathered = lax.all_gather(rounded, "island", axis=1, tiled=True)
        fresh = jnp.where(myself == source, gathered, fresh)
    return (fresh[None], theta, momentum, accum)


def solution(mesh):
    placed = (
        P("island", "expert", "fsdp", None),
        P(),
        P(),
        P(),
        P(),
        P("expert", ("fsdp", "island"), None),
        P("expert", ("fsdp", "island"), None),
        P("expert", ("fsdp", "island"), None),
    )
    return jax.shard_map(
        local,
        mesh=mesh,
        in_specs=placed,
        out_specs=(
            P("island", "expert", "fsdp", None),
            P("expert", ("fsdp", "island"), None),
            P("expert", ("fsdp", "island"), None),
            P("expert", ("fsdp", "island"), None),
        ),
        check_vma=False,
    )
```

profile of v0, /device:TPU:24, one launch (start us, length us, event | category | flops | bytes accessed | tf_op | source)
XLA Modules:
  0.0 954.0 jit_solution(10924398924033915100)
XLA Ops:
  7.2 0.0 all-reduce.3.cloned.1.call-start
  7.2 1.5 fusion.5
  11.3 6.2 select_bitcast_fusion.1
  17.4 0.0 copy-start.3
  17.4 0.0 copy-start
  17.4 0.0 copy-start.1
  17.4 0.0 copy-start.2
  17.4 0.0 all-reduce.3.cloned.1.call-update
  17.5 0.0 all-gather.5.cloned.1.call-start
  26.6 0.0 copy-done.3
  26.7 0.7 fusion.4
  30.4 537.1 %all-reduce.3.cloned.1.call-done = (bf16[1,1024,1536]{2,1,0:T(8,128)(2,1)}, bf16[1,1024,1536]{2,1,0:T(8,128)(2,1)}, bf16[1,1024,1536]{2,1,0:T(8,128)(2,1)}, bf16[1,1024,1536]{2,1,0:T(8,128)(2,1)}) async-done(((bf16[1,1024,1536]{2,1,0:T(8,128)(2,1)}, bf16[1,1024,1536]{2,1,0:T(8,128)(2,1)}, bf16[1,1024,1536]{2,1,0:T(8,128)(2,1)}, bf16[1,1024,1536]{2,1,0:T(8,128)(2,1)}), (bf16[1,1024,1536]{2,1,0:T(8,128)(2,1)}, ...) | async-done | bytes 12582928 | tf_op jit(solution)/shard_map/psum | solution.py:9
  567.5 0.0 copy-done
  567.5 0.0 copy-done.1
  567.5 0.0 copy-done.2
  567.5 1.8 fusion.1
  569.3 2.4 add_select_fusion
  571.7 2.0 fusion.2
  573.7 2.2 fusion.3
  575.9 0.0 all-gather.5.cloned.1.call-update
  575.9 0.0 all-gather.7.cloned.1.call-start
  576.0 0.7 all-gather.7.cloned.1.call-update
  576.6 0.0 all-gather.9.cloned.1.call-start
  576.7 0.5 all-gather.9.cloned.1.call-update
  577.2 0.0 all-gather.11.cloned.1.call-start
  577.3 0.5 all-gather.11.cloned.1.call-update
  577.8 90.3 %all-gather.5.cloned.1.call-done = bf16[1,1024,1536]{2,1,0:T(8,128)(2,1)} async-done(((bf16[1,64,1536]{2,1,0:T(8,128)(2,1)}), bf16[1,1024,1536]{2,1,0:T(8,128)(2,1)}) %all-gather.5.cloned.1.call-update) | async-done | bytes 3145744 | tf_op jit(solution)/shard_map/all_gather | solution.py:36
  668.1 91.7 %all-gather.7.cloned.1.call-done = bf16[1,1024,1536]{2,1,0:T(8,128)(2,1)} async-done(((bf16[1,64,1536]{2,1,0:T(8,128)(2,1)}), bf16[1,1024,1536]{2,1,0:T(8,128)(2,1)}) %all-gather.7.cloned.1.call-update) | async-done | bytes 3145744 | tf_op jit(solution)/shard_map/all_gather | solution.py:36
  759.8 91.5 %all-gather.9.cloned.1.call-done = bf16[1,1024,1536]{2,1,0:T(8,128)(2,1)} async-done(((bf16[1,64,1536]{2,1,0:T(8,128)(2,1)}), bf16[1,1024,1536]{2,1,0:T(8,128)(2,1)}) %all-gather.9.cloned.1.call-update) | async-done | bytes 3145744 | tf_op jit(solution)/shard_map/all_gather | solution.py:36
  851.3 92.1 %all-gather.11.cloned.1.call-done = bf16[1,1024,1536]{2,1,0:T(8,128)(2,1)} async-done(((bf16[1,64,1536]{2,1,0:T(8,128)(2,1)}), bf16[1,1024,1536]{2,1,0:T(8,128)(2,1)}) %all-gather.11.cloned.1.call-update) | async-done | bytes 3145744 | tf_op jit(solution)/shard_map/all_gather | solution.py:36
  943.4 4.1 select_bitcast_fusion
Async XLA Ops:
  7.2 560.3 %all-reduce.3.cloned.1.call-start = ((), (), s32[]{:S(2)}) async-start(), calls=%async_computation.4 | async-start | bytes 25165824 | tf_op jit(solution)/shard_map/psum | solution.py:9
  17.4 9.2 copy-start.3
  17.4 550.1 %copy-start = (f32[1,64,1536]{2,1,0:T(8,128)S(1)}, f32[1,64,1536]{2,1,0:T(8,128)}, u32[]{:S(2)}) copy-start(f32[1,64,1536]{2,1,0:T(8,128)} %param.15) | copy-start | bytes 1179652
  17.4 550.1 %copy-start.1 = (f32[1,64,1536]{2,1,0:T(8,128)S(1)}, f32[1,64,1536]{2,1,0:T(8,128)}, u32[]{:S(2)}) copy-start(f32[1,64,1536]{2,1,0:T(8,128)} %param.14) | copy-start | bytes 1179652
  17.4 550.1 %copy-start.2 = (f32[1,64,1536]{2,1,0:T(8,128)S(1)}, f32[1,64,1536]{2,1,0:T(8,128)}, u32[]{:S(2)}) copy-start(f32[1,64,1536]{2,1,0:T(8,128)} %param.13) | copy-start | bytes 1179652
  17.5 650.6 %all-gather.5.cloned.1.call-start = ((), (), s32[]{:S(2)}) async-start(), calls=%async_computation | async-start | bytes 3342336 | tf_op jit(solution)/shard_map/all_gather | solution.py:36
  575.9 183.9 %all-gather.7.cloned.1.call-start = ((), (), s32[]{:S(2)}) async-start(), calls=%async_computation.1 | async-start | bytes 3342336 | tf_op jit(solution)/shard_map/all_gather | solution.py:36
  576.6 274.6 %all-gather.9.cloned.1.call-start = ((), (), s32[]{:S(2)}) async-start(), calls=%async_computation.2 | async-start | bytes 3342336 | tf_op jit(solution)/shard_map/all_gather | solution.py:36
  577.2 366.2 %all-gather.11.cloned.1.call-start = ((), (), s32[]{:S(2)}) async-start(), calls=%async_computation.3 | async-start | bytes 3342336 | tf_op jit(solution)/shard_map/all_gather | solution.py:36
Sparse Core Ops, SparseCore 0:
  17.6 549.8 all-reduce.2
  576.0 92.0 all-gather.4
  669.9 89.8 all-gather.6
  761.4 89.8 all-gather.8
  853.5 89.8 all-gather.10
where the time goes:
time: 954 us
  waiting for transfers between devices  904 us (95%)
  between operations  28.5 us (3%)
  other arithmetic  18.7 us (2%)
    psum x1, waiting for transfers between devices, spread(): return lax.psum(jnp.where(mine, shard, jnp.zeros_like(shard)), axis)  537 us
    all_gather x4, waiting for transfers between devices, local(): gathered = lax.all_gather(rounded, 'island', axis=1, tiled=True)  366 us
  transfers between devices with their start and end apart: 5, of which 5 were waited for; matrix products, arithmetic and copies ran while one was open for 0% of the time, Pallas kernels for 0%

commit v1 on v0

--- a/solution.py
+++ b/solution.py
@@ -33,7 +33,8 @@
             grad + jnp.where(boundary, beta * momentum / correction, jnp.float32(0.0))
         )
         rounded = theta.astype(jnp.bfloat16)
-        gathered = lax.all_gather(rounded, "island", axis=1, tiled=True)
+        outgoing = jnp.stack([rounded] * lax.axis_size("island"))
+        gathered = jnp.concatenate(lax.all_to_all(outgoing, "island", 0, 0), axis=1)
         fresh = jnp.where(myself == source, gathered, fresh)
     return (fresh[None], theta, momentum, accum)
 

time: 954 us -> 888 us (0.931)
  waiting for transfers between devices: 904 us -> 537 us
  blocking collectives: 0 us -> 303 us
    all_gather x4 -> x0, waiting for transfers between devices: 366 us -> none  [local(): gathered = lax.all_gather(rounded, 'island', axis=1, tiled=True)]
    all_to_all x0 -> x4, blocking collectives: none -> 303 us  [local(): gathered = jnp.concatenate(lax.all_to_all(outgoing, 'island', 0, 0), axis=1)]
  transfers between devices with their start and end apart: 5 -> 1, of which waited for: 5 -> 1; matrix products, arithmetic and copies ran while one was open for 0% -> 0% of each run, Pallas kernels for 0% -> 0%
where the time goes in v1:
time: 888 us
  waiting for transfers between devices  537 us (60%)
  blocking collectives  303 us (34%)
  between operations  28.7 us (3%)
  other arithmetic  15.3 us (2%)
    psum x1, waiting for transfers between devices, spread(): return lax.psum(jnp.where(mine, shard, jnp.zeros_like(shard)), axis)  537 us
    all_to_all x4, blocking collectives, local(): gathered = jnp.concatenate(lax.all_to_all(outgoing, 'island', 0, 0), axis=1)  303 us
  transfers between devices with their start and end apart: 1, of which 1 were waited for; matrix products, arithmetic and copies ran while one was open for 0% of the time, Pallas kernels for 0%

profile of v1, /device:TPU:24, one launch (start us, length us, event | category | flops | bytes accessed | tf_op | source)
XLA Modules:
  0.0 887.6 jit_solution(2729028770447125908)
XLA Ops:
  7.2 0.0 all-reduce.3.cloned.1.call-start
  7.2 1.5 fusion.1
  11.2 6.1 select_bitcast_fusion
  17.4 0.0 copy-start.3
  17.4 0.0 copy-start
  17.4 0.0 copy-start.1
  17.4 0.0 copy-start.2
  17.4 0.0 all-reduce.3.cloned.1.call-update
  26.5 0.0 copy-done.3
  26.5 0.7 fusion
  30.2 537.2 %all-reduce.3.cloned.1.call-done = (bf16[1,1024,1536]{2,1,0:T(8,128)(2,1)}, bf16[1,1024,1536]{2,1,0:T(8,128)(2,1)}, bf16[1,1024,1536]{2,1,0:T(8,128)(2,1)}, bf16[1,1024,1536]{2,1,0:T(8,128)(2,1)}) async-done(((bf16[1,1024,1536]{2,1,0:T(8,128)(2,1)}, bf16[1,1024,1536]{2,1,0:T(8,128)(2,1)}, bf16[1,1024,1536]{2,1,0:T(8,128)(2,1)}, bf16[1,1024,1536]{2,1,0:T(8,128)(2,1)}), (bf16[1,1024,1536]{2,1,0:T(8,128)(2,1)}, ...) | async-done | bytes 12582928 | tf_op jit(solution)/shard_map/psum | solution.py:9
  567.4 0.0 copy-done
  567.4 0.0 copy-done.1
  567.4 0.0 copy-done.2
  567.4 1.1 convert_bitcast_fusion
  568.5 2.4 add_select_fusion
  570.9 1.3 convert_bitcast_fusion.2
  572.2 2.2 convert_bitcast_fusion.3
  574.4 0.3 stack.8
  574.7 77.1 %all_to_all.20 = bf16[16,1,64,1536]{3,2,1,0:T(8,128)(2,1)S(1)} all-to-all(bf16[16,1,64,1536]{3,2,1,0:T(8,128)(2,1)S(1)} %stack.8), channel_id=1, replica_groups=mesh['island'=16,'expert'=4,'fsdp'=4] {'island'}, dimensions={0} | all-to-all | bytes 6291456 | tf_op jit(solution)/shard_map/all_to_all | solution.py:37
  651.8 0.3 stack.9
  652.1 75.5 %all_to_all.21 = bf16[16,1,64,1536]{3,2,1,0:T(8,128)(2,1)S(1)} all-to-all(bf16[16,1,64,1536]{3,2,1,0:T(8,128)(2,1)S(1)} %stack.9), channel_id=1, replica_groups=mesh['island'=16,'expert'=4,'fsdp'=4] {'island'}, dimensions={0} | all-to-all | bytes 6291456 | tf_op jit(solution)/shard_map/all_to_all | solution.py:37
  727.6 0.3 stack.10
  727.9 75.2 %all_to_all.22 = bf16[16,1,64,1536]{3,2,1,0:T(8,128)(2,1)S(1)} all-to-all(bf16[16,1,64,1536]{3,2,1,0:T(8,128)(2,1)S(1)} %stack.10), channel_id=1, replica_groups=mesh['island'=16,'expert'=4,'fsdp'=4] {'island'}, dimensions={0} | all-to-all | bytes 6291456 | tf_op jit(solution)/shard_map/all_to_all | solution.py:37
  803.1 0.3 stack.11
  803.4 75.1 %all_to_all.23 = bf16[16,1,64,1536]{3,2,1,0:T(8,128)(2,1)S(1)} all-to-all(bf16[16,1,64,1536]{3,2,1,0:T(8,128)(2,1)S(1)} %stack.11), channel_id=1, replica_groups=mesh['island'=16,'expert'=4,'fsdp'=4] {'island'}, dimensions={0} | all-to-all | bytes 6291456 | tf_op jit(solution)/shard_map/all_to_all | solution.py:37
  878.5 2.2 select_select_fusion
Async XLA Ops:
  7.2 560.2 %all-reduce.3.cloned.1.call-start = ((), (), s32[]{:S(2)}) async-start(), calls=%async_computation.4 | async-start | bytes 25165824 | tf_op jit(solution)/shard_map/psum | solution.py:9
  17.4 9.2 %copy-start.3 = (s32[16]{0:T(128)S(1)}, s32[16]{0:T(128)}, u32[]{:S(2)}) copy-start(s32[16]{0:T(128)} %param.10) | copy-start | bytes 196
  17.4 550.1 %copy-start = (f32[1,64,1536]{2,1,0:T(8,128)S(1)}, f32[1,64,1536]{2,1,0:T(8,128)}, u32[]{:S(2)}) copy-start(f32[1,64,1536]{2,1,0:T(8,128)} %param.15) | copy-start | bytes 1179652
  17.4 550.1 %copy-start.1 = (f32[1,64,1536]{2,1,0:T(8,128)S(1)}, f32[1,64,1536]{2,1,0:T(8,128)}, u32[]{:S(2)}) copy-start(f32[1,64,1536]{2,1,0:T(8,128)} %param.14) | copy-start | bytes 1179652
  17.4 550.1 %copy-start.2 = (f32[1,64,1536]{2,1,0:T(8,128)S(1)}, f32[1,64,1536]{2,1,0:T(8,128)}, u32[]{:S(2)}) copy-start(f32[1,64,1536]{2,1,0:T(8,128)} %param.13) | copy-start | bytes 1179652
Sparse Core Ops, SparseCore 0:
  17.5 549.8 all-reduce.2
